TPU v7x, 32 devices: a whole 2x2x4 slice. The times are simulated.
32 devices in a mesh: prow: 4 (over y, core), pcol: 8 (over z, x).
Axes of the slice: x: 2, y: 2, z: 4, core: 2. Of those that a mesh axis runs over, the one named last changes fastest.
Arguments:
- matrix: float32 [10240, 9216], P('prow', 'pcol'), as said below
- pivots: int32 [1024], replicated, may hold values from 0 to 10239, as said below
Outputs:
- updated: float32 [10240, 9216], P('prow', 'pcol')
Inputs may be any that keep to these rules, and one draw needn't show every extreme that they name: For each i < 1024, pivots[i] is i or a row index of 1024 or more; indices of 1024 or more are distinct. `matrix`: the first 1024 columns hold the factored panel: below the diagonal, the multipliers of the lower factor.
All inputs are finite; a program needn't handle non-finite values.
Results may differ from a plain program's by a relative error of at most 0.000051.
Values sent between devices are 32-bit elements; how exact they have to be, the bound alone decides.
A program may use at most 128 MiB of HBM per device.

v0:
```python
import jax
import jax.numpy as jnp
from jax import lax
from jax.sharding import PartitionSpec as P


def spread(block, axis, owner):
    block = jnp.where(lax.axis_index(axis) == owner, block, jnp.zeros_like(block))
    return lax.psum(block, axis)


def on_device(matrix, pivots):
    row_count = matrix.shape[0]
    col_count = matrix.shape[1]
    panel_width = pivots.shape[0]
    prow_index = lax.axis_index("prow")
    pcol_index = lax.axis_index("pcol")
    panel_rows = spread(matrix[:, :panel_width], "pcol", 0)
    pieces = ((panel_rows, 0, panel_width),)
    owner_prow = pivots // row_count
    local_row = pivots - owner_prow * row_count
    is_mine = (owner_prow == prow_index)[:, None]
    contribution = jnp.where(is_mine, matrix[local_row], 0.0)
    new_top = lax.psum(contribution, "prow")
    old_top = spread(matrix[:panel_width], "prow", 0)

    def solve_top(top_rows):
        return lax.linalg.triangular_solve(
            panel_rows[:panel_width], top_rows, left_side=True, lower=True, unit_diagonal=True
        )

    solved = lax.cond(prow_index == 0, solve_top, jnp.zeros_like, new_top)
    upper_rows = spread(solved, "prow", 0)
    destination = jnp.where(
        (owner_prow == prow_index) & (pivots >= panel_width), local_row, row_count
    )
    swapped = matrix.at[destination].set(old_top, mode="drop")
    piece, begin, finish = pieces[0]
    product = jnp.dot(
        piece, upper_rows, precision=lax.Precision.HIGHEST, preferred_element_type=jnp.float32
    )
    result = swapped - product
    padded_upper = jnp.concatenate(
        [upper_rows, jnp.zeros((row_count - panel_width, col_count), jnp.float32)], axis=0
    )
    global_row = prow_index * row_count + lax.broadcasted_iota(jnp.int32, (row_count, 1), 0)
    result = jnp.where(global_row < panel_width, padded_upper, result)
    global_col = pcol_index * col_count + lax.broadcasted_iota(jnp.int32, (1, col_count), 1)
    return jnp.where(global_col < panel_width, matrix, result)


def solution(mesh):
    return jax.shard_map(
        on_device,
        mesh=mesh,
        in_specs=(P("prow", "pcol"), P()),
        out_specs=P("prow", "pcol"),
        check_vma=False,
    )
```

profile of v0, /device:TPU:0, one launch (start us, length us, event | category | flops | bytes accessed | tf_op | source)
XLA Modules:
  0.0 838.4 jit_solution(6654059166047416843)
XLA Ops:
  6.5 0.7 fusion.35
  7.2 0.7 broadcast_compare_fusion
  7.9 11.0 %gather_fusion = f32[1024,1152]{1,0:T(8,128)} fusion(f32[2560,1152]{1,0:T(8,128)} %param.4, s32[1024]{0:T(1024)S(1)} %get-tuple-element.63), kind=kCustom, calls=%fused_computation | custom fusion | bytes 9441280 | tf_op jit(solution)/shard_map/gather | solution.py:23
  19.0 4.8 broadcast_select_fusion.1
  23.9 10.8 %slice_select_fusion = f32[2560,1024]{1,0:T(8,128)} fusion(f32[2560,1152]{1,0:T(8,128)} %param.4, pred[]{:T(512)S(6)} %eq.17), kind=kLoop, calls=%fused_computation.86 | loop fusion | flops 2621440 | bytes 20971520 | tf_op jit(solution)/shard_map/jit(_where)/select_n | solution.py:8
  34.7 4.8 slice_select_fusion.1
  39.6 81.1 %all-reduce.8.cloned.1.call-done = f32[1024,1152]{1,0:T(8,128)} async-done(((f32[1024,1152]{1,0:T(8,128)}), f32[1024,1152]{1,0:T(8,128)}) %all-reduce.8.cloned.1.call-update) | async-done | bytes 4718608 | tf_op jit(solution)/shard_map/psum | solution.py:24
  120.7 331.4 %all-reduce.6.cloned.1.call-done = f32[2560,1024]{1,0:T(8,128)} async-done(((f32[2560,1024]{1,0:T(8,128)}), f32[2560,1024]{1,0:T(8,128)}) %all-reduce.6.cloned.1.call-update) | async-done | bytes 10485776 | tf_op jit(solution)/shard_map/psum | solution.py:9
  452.1 138.6 %conditional.1 = (f32[1024,1152]{1,0:T(8,128)}) conditional(s32[]{:T(128)} %convert_element_type.3, () %tuple.11, (f32[2560,1024]{1,0:T(8,128)}, f32[1024,1152]{1,0:T(8,128)}) %tuple.12), branch_computations={%region_2.3_spmd, %region_3.4_spmd} | conditional | flops 8162952192 | bytes 76947776 | solution.py:32
  452.1 4.6 convert_add_fusion
  456.7 23.3 %while.1 = (s32[]{:T(128)}, f32[1024,1024]{1,0:T(8,128)}, s32[8,2]{0,1:T(2,128)S(1)}, f32[8,128,128]{2,1,0:T(8,128)S(1)}, s32[]{:T(128)}) while((s32[]{:T(128)}, f32[1024,1024]{1,0:T(8,128)}, s32[8,2]{0,1:T(2,128)S(1)}, f32[8,128,128]{2,1,0:T(8,128)S(1)}, s32[]{:T(128)}) %tuple.50), condition=%wide.while_cond, body=%wide.while_body.sunk | while | flops 2 | bytes 131181 | solution.py:28
  456.7 0.6 fusion.52
  457.3 2.2 bitcast_dynamic-update-slice_fusion.2
  459.7 0.6 fusion.52
  460.3 2.2 bitcast_dynamic-update-slice_fusion.2
  462.6 0.6 fusion.52
  463.2 2.2 bitcast_dynamic-update-slice_fusion.2
  465.5 0.6 fusion.52
  466.1 2.2 bitcast_dynamic-update-slice_fusion.2
  468.5 0.6 fusion.52
  469.1 2.2 bitcast_dynamic-update-slice_fusion.2
  471.4 0.6 fusion.52
  472.0 2.2 bitcast_dynamic-update-slice_fusion.2
  474.3 0.6 fusion.52
  474.9 2.2 bitcast_dynamic-update-slice_fusion.2
  477.2 0.6 fusion.52
  477.8 2.2 bitcast_dynamic-update-slice_fusion.2
  480.0 78.8 %custom-call.2 = f32[8,128,128]{1,2,0:T(8,128)S(1)} custom-call(f32[8,128,128]{2,1,0:T(8,128)S(1)} %get-tuple-element.21), custom_call_target="InvertDiagBlocksLowerTriangular" | custom-call | tf_op jit(solution)/shard_map/cond/branch_1_fun/triangular_solve | solution.py:28
  558.8 2.8 constant_dynamic-update-slice_fusion.17
  561.6 1.7 convolution_subtract_fusion.6
  563.3 1.6 constant_dynamic-update-slice_fusion.16
  565.0 1.7 convolution_subtract_fusion.5
  566.7 1.6 constant_dynamic-update-slice_fusion.15
  568.3 2.2 convolution_subtract_fusion.2
  570.5 1.6 constant_dynamic-update-slice_fusion.14
  572.1 2.4 convolution_subtract_fusion.4
  574.6 1.5 constant_dynamic-update-slice_fusion.13
  576.1 3.0 convolution_subtract_fusion
  579.1 1.5 constant_dynamic-update-slice_fusion.12
  580.6 3.4 convolution_subtract_fusion.1
  584.0 1.5 constant_dynamic-update-slice_fusion.11
  585.5 3.7 convolution_subtract_fusion.3
  589.2 1.5 convolution_dynamic-update-slice_fusion
  590.7 4.8 broadcast_select_fusion
  595.5 10.4 %copy.38 = f32[2560,1152]{1,0:T(8,128)} copy(f32[2560,1152]{1,0:T(8,128)} %param.4) | data formatting | bytes 23592960
  605.9 158.1 %all-reduce.10.cloned.1.call-done = (f32[1024,1152]{1,0:T(8,128)}, f32[1024,1152]{1,0:T(8,128)}) async-done(((f32[1024,1152]{1,0:T(8,128)}, f32[1024,1152]{1,0:T(8,128)}), (f32[1024,1152]{1,0:T(8,128)}, f32[1024,1152]{1,0:T(8,128)})) %all-reduce.10.cloned.1.call-update) | async-done | bytes 9437200 | tf_op jit(solution)/shard_map/psum | solution.py:9
  763.9 15.0 %scatter_fusion = f32[2560,1152]{1,0:T(8,128)} fusion(f32[2560,1152]{1,0:T(8,128)} %copy.38, s32[1024]{0:T(1024)S(1)} %get-tuple-element.64, f32[1024,1152]{1,0:T(8,128)} %get-tuple-element.30), kind=kCustom, calls=%fused_computation.1 | custom fusion | bytes 14159872 | tf_op jit(solution)/shard_map/scatter | solution.py:37
  778.9 53.0 %fusion.34 = f32[2560,1152]{1,0:T(8,128)} fusion(f32[2560,1152]{1,0:T(8,128)} %param.4, f32[2560,1152]{1,0:T(8,128)} %scatter_fusion, f32[2560,1024]{1,0:T(8,128)} %all-reduce.6.cloned.1.call-done, f32[1024,1152]{1,0:T(8,128)} %get-tuple-element.31, pred[2560]{0:T(1024)(128)(4,1)S(1)} %add_compare_fusion, pred[1152]{0:T(1024)(128)(4,1)S(1)} %add_compare_fusion.1), kind=kOutput, calls=%fused_computation.85 | convolution fusion | flops 36247633920 | bytes 50597504 | tf_op jit(solution)/shard_map/dot_general | solution.py:39
  (22 shorter events, 0.8 us)
Async XLA Ops:
  6.5 114.2 %all-reduce.8.cloned.1.call-start = ((), (), s32[]{:S(2)}) async-start(), calls=%async_computation.1 | async-start | bytes 9437184 | tf_op jit(solution)/shard_map/psum | solution.py:24
  23.8 428.3 %all-reduce.6.cloned.1.call-start = ((), (), s32[]{:S(2)}) async-start(), calls=%async_computation | async-start | bytes 20971520 | tf_op jit(solution)/shard_map/psum | solution.py:9
  34.7 729.3 %all-reduce.10.cloned.1.call-start = ((), (), s32[]{:S(2)}) async-start(), calls=%async_computation.2 | async-start | bytes 18874368 | tf_op jit(solution)/shard_map/psum | solution.py:9
  558.8 6.2 copy-start
Sparse Core Ops, SparseCore 0:
  23.9 96.7 all-reduce.7
  124.6 327.4 all-reduce.5
  595.6 168.2 all-reduce.9
where the time goes:
time: 839 us; the launch traced here: 838 us
  waiting for transfers between devices  571 us (68%)
  other arithmetic  110 us (13%)
  matrix products  84.9 us (10%)
  local copies, waits for them, and re-layouts  59.5 us (7%)
  between operations  13.1 us (2%)
    psum x2, waiting for transfers between devices, spread(): return lax.psum(block, axis)  489 us
    another operation x4, other arithmetic, solve_top(): lax.linalg.triangular_solve(panel_rows[:panel_width], top_rows, left_side...  83.4 us
    psum x1, waiting for transfers between devices, on_device(): new_top = lax.psum(contribution, 'prow')  81.1 us
    dot_general x1, matrix products, on_device(): jnp.dot(piece, upper_rows, precision=lax.Precision.HIGHEST, preferred_ele...  53 us
    another operation x15, matrix products, solve_top(): lax.linalg.triangular_solve(panel_rows[:panel_width], top_rows, left_side...  31.9 us
    another operation x24, local copies, waits for them, and re-layouts  23.2 us
    select_n x3, other arithmetic, spread(): jnp.where(lax.axis_index(axis) == owner, block, jnp.zeros_like(block))  20.4 us
  transfers between devices with their start and end apart: 3, of which 3 were waited for; matrix products, arithmetic and copies ran while one was open for 3% of the time, Pallas kernels for 0%

commit v1 on v0

--- a/solution.py
+++ b/solution.py
@@ -21,7 +21,7 @@
     local_row = pivots - owner_prow * row_count
     is_mine = (owner_prow == prow_index)[:, None]
     contribution = jnp.where(is_mine, matrix[local_row], 0.0)
-    new_top = lax.psum(contribution, "prow")
+    new_top = jnp.sum(lax.all_gather(contribution, "prow"), axis=0)
     old_top = spread(matrix[:panel_width], "prow", 0)
 
     def solve_top(top_rows):

time: 839 us -> 762 us (0.908)
  waiting for transfers between devices: 571 us -> 473 us
  other arithmetic: 110 us -> 122 us
    psum x2, waiting for transfers between devices: 489 us -> 367 us  [spread(): return lax.psum(block, axis)]
    all_gather x0 -> x1, waiting for transfers between devices: none -> 106 us  [on_device(): new_top = jnp.sum(lax.all_gather(contribution, 'prow'), axis=0)]
    psum x1 -> x0, waiting for transfers between devices: 81.1 us -> none  [on_device(): new_top = lax.psum(contribution, 'prow')]
    reduce_sum x0 -> x1, other arithmetic: none -> 10.2 us  [on_device(): new_top = jnp.sum(lax.all_gather(contribution, 'prow'), axis=0)]
  transfers between devices with their start and end apart: 3 -> 3, of which waited for: 3 -> 3; matrix products, arithmetic and copies ran while one was open for 3% -> 5% of each run, Pallas kernels for 0% -> 0%
where the time goes in v1:
time: 762 us; the launch traced here: 755 us
  waiting for transfers between devices  473 us (62%)
  other arithmetic  122 us (16%)
  matrix products  85.2 us (11%)
  local copies, waits for them, and re-layouts  59.5 us (8%)
  between operations  15.1 us (2%)
    psum x2, waiting for transfers between devices, spread(): return lax.psum(block, axis)  367 us
    all_gather x1, waiting for transfers between devices, on_device(): new_top = jnp.sum(lax.all_gather(contribution, 'prow'), axis=0)  106 us
    another operation x4, other arithmetic, solve_top(): lax.linalg.triangular_solve(panel_rows[:panel_width], top_rows, left_side...  83.4 us
    dot_general x1, matrix products, on_device(): jnp.dot(piece, upper_rows, precision=lax.Precision.HIGHEST, preferred_ele...  53.1 us
    another operation x15, matrix products, solve_top(): lax.linalg.triangular_solve(panel_rows[:panel_width], top_rows, left_side...  32.1 us
    another operation x24, local copies, waits for them, and re-layouts  23 us
    select_n x3, other arithmetic, spread(): jnp.where(lax.axis_index(axis) == owner, block, jnp.zeros_like(block))  21.9 us
  transfers between devices with their start and end apart: 3, of which 3 were waited for; matrix products, arithmetic and copies ran while one was open for 5% of the time, Pallas kernels for 0%

profile of v1, /device:TPU:0, one launch (start us, length us, event | category | flops | bytes accessed | tf_op | source)
XLA Modules:
  0.0 754.9 jit_solution(2111273828710288298)
XLA Ops:
  7.4 0.7 fusion.35
  8.1 0.7 broadcast_compare_fusion
  8.8 11.0 %gather_fusion = f32[1024,1152]{1,0:T(8,128)} fusion(f32[2560,1152]{1,0:T(8,128)} %param.4, s32[1024]{0:T(1024)S(1)} %get-tuple-element.63), kind=kCustom, calls=%fused_computation | custom fusion | bytes 9441280 | tf_op jit(solution)/shard_map/gather | solution.py:23
  19.8 5.0 bitcast_select_fusion
  24.8 11.2 %slice_select_fusion = f32[2560,1024]{1,0:T(8,128)} fusion(f32[2560,1152]{1,0:T(8,128)} %param.4, pred[]{:T(512)S(6)} %eq.17), kind=kLoop, calls=%fused_computation.86 | loop fusion | flops 2621440 | bytes 20971520 | tf_op jit(solution)/shard_map/jit(_where)/select_n | solution.py:8
  36.2 5.8 slice_select_fusion.1
  42.0 105.7 %all-gather.2.cloned.1.call-done = f32[4,1024,1152]{2,1,0:T(8,128)} async-done(((f32[1,1024,1152]{2,1,0:T(8,128)}), f32[4,1024,1152]{2,1,0:T(8,128)}) %all-gather.2.cloned.1.call-update) | async-done | bytes 18874384 | tf_op jit(solution)/shard_map/all_gather | solution.py:24
  147.7 10.2 %reduce_sum.9 = f32[1024,1152]{1,0:T(8,128)} reduce(f32[4,1024,1152]{2,1,0:T(8,128)} %all-gather.2.cloned.1.call-done, f32[]{:T(128)} %constant.41.clone.1), dimensions={0}, to_apply=%region_1.2 | reduce | flops 3538944 | bytes 23592964 | tf_op jit(solution)/shard_map/reduce_sum | solution.py:24
  157.9 208.8 %all-reduce.5.cloned.1.call-done = f32[2560,1024]{1,0:T(8,128)} async-done(((f32[2560,1024]{1,0:T(8,128)}), f32[2560,1024]{1,0:T(8,128)}) %all-reduce.5.cloned.1.call-update) | async-done | bytes 10485776 | tf_op jit(solution)/shard_map/psum | solution.py:9
  366.6 139.0 %conditional.1 = (f32[1024,1152]{1,0:T(8,128)}) conditional(s32[]{:T(128)} %convert_element_type.3, () %tuple.11, (f32[2560,1024]{1,0:T(8,128)}, f32[1024,1152]{1,0:T(8,128)}) %tuple.12), branch_computations={%region_2.3_spmd, %region_3.4_spmd} | conditional | flops 8162952192 | bytes 76947776 | solution.py:32
  366.6 4.5 convert_add_fusion
  371.2 23.2 %while.1 = (s32[]{:T(128)}, f32[1024,1024]{1,0:T(8,128)}, s32[8,2]{0,1:T(2,128)S(1)}, f32[8,128,128]{2,1,0:T(8,128)S(1)}, s32[]{:T(128)}) while((s32[]{:T(128)}, f32[1024,1024]{1,0:T(8,128)}, s32[8,2]{0,1:T(2,128)S(1)}, f32[8,128,128]{2,1,0:T(8,128)S(1)}, s32[]{:T(128)}) %tuple.50), condition=%wide.while_cond, body=%wide.while_body.sunk | while | flops 2 | bytes 131181 | solution.py:28
  371.8 2.2 bitcast_dynamic-update-slice_fusion.2
  374.1 0.6 fusion.52
  374.7 2.2 bitcast_dynamic-update-slice_fusion.2
  377.1 0.6 fusion.52
  377.6 2.2 bitcast_dynamic-update-slice_fusion.2
  380.0 0.6 fusion.52
  380.5 2.2 bitcast_dynamic-update-slice_fusion.2
  382.9 0.6 fusion.52
  383.5 2.2 bitcast_dynamic-update-slice_fusion.2
  385.8 0.6 fusion.52
  386.4 2.2 bitcast_dynamic-update-slice_fusion.2
  388.7 0.6 fusion.52
  389.3 2.2 bitcast_dynamic-update-slice_fusion.2
  391.6 0.6 fusion.52
  392.2 2.2 bitcast_dynamic-update-slice_fusion.2
  394.3 78.9 %custom-call.2 = f32[8,128,128]{1,2,0:T(8,128)S(1)} custom-call(f32[8,128,128]{2,1,0:T(8,128)S(1)} %get-tuple-element.21), custom_call_target="InvertDiagBlocksLowerTriangular" | custom-call | tf_op jit(solution)/shard_map/cond/branch_1_fun/triangular_solve | solution.py:28
  473.3 2.8 constant_dynamic-update-slice_fusion.17
  476.1 1.7 convolution_subtract_fusion.6
  477.8 1.6 constant_dynamic-update-slice_fusion.16
  479.4 1.7 convolution_subtract_fusion.5
  481.1 1.6 constant_dynamic-update-slice_fusion.15
  482.7 2.2 convolution_subtract_fusion.2
  485.0 1.6 constant_dynamic-update-slice_fusion.14
  486.6 2.4 convolution_subtract_fusion.4
  489.0 1.5 constant_dynamic-update-slice_fusion.13
  490.6 3.0 convolution_subtract_fusion
  493.5 1.5 constant_dynamic-update-slice_fusion.12
  495.0 3.7 convolution_subtract_fusion.1
  498.8 1.5 constant_dynamic-update-slice_fusion.11
  500.3 3.7 convolution_subtract_fusion.3
  503.9 1.5 convolution_dynamic-update-slice_fusion
  505.6 4.9 broadcast_select_fusion
  510.5 10.3 %copy.37 = f32[2560,1152]{1,0:T(8,128)} copy(f32[2560,1152]{1,0:T(8,128)} %param.4) | data formatting | bytes 23592960
  520.9 158.1 %all-reduce.7.cloned.1.call-done = (f32[1024,1152]{1,0:T(8,128)}, f32[1024,1152]{1,0:T(8,128)}) async-done(((f32[1024,1152]{1,0:T(8,128)}, f32[1024,1152]{1,0:T(8,128)}), (f32[1024,1152]{1,0:T(8,128)}, f32[1024,1152]{1,0:T(8,128)})) %all-reduce.7.cloned.1.call-update) | async-done | bytes 9437200 | tf_op jit(solution)/shard_map/psum | solution.py:9
  679.0 15.1 %scatter_fusion = f32[2560,1152]{1,0:T(8,128)} fusion(f32[2560,1152]{1,0:T(8,128)} %copy.37, s32[1024]{0:T(1024)S(1)} %get-tuple-element.64, f32[1024,1152]{1,0:T(8,128)} %get-tuple-element.30), kind=kCustom, calls=%fused_computation.1 | custom fusion | bytes 14159872 | tf_op jit(solution)/shard_map/scatter | solution.py:37
  694.1 53.1 %fusion.34 = f32[2560,1152]{1,0:T(8,128)} fusion(f32[2560,1152]{1,0:T(8,128)} %param.4, f32[2560,1152]{1,0:T(8,128)} %scatter_fusion, f32[2560,1024]{1,0:T(8,128)} %all-reduce.5.cloned.1.call-done, f32[1024,1152]{1,0:T(8,128)} %get-tuple-element.31, pred[2560]{0:T(1024)(128)(4,1)S(1)} %add_compare_fusion, pred[1152]{0:T(1024)(128)(4,1)S(1)} %add_compare_fusion.1), kind=kOutput, calls=%fused_computation.85 | convolution fusion | flops 36247633920 | bytes 50597504 | tf_op jit(solution)/shard_map/dot_general | solution.py:39
  (23 shorter events, 1.3 us)
Async XLA Ops:
  7.4 140.3 %all-gather.2.cloned.1.call-start = ((), (), s32[]{:S(2)}) async-start(), calls=%async_computation.1 | async-start | bytes 23592960 | tf_op jit(solution)/shard_map/all_gather | solution.py:24
  24.8 341.8 %all-reduce.5.cloned.1.call-start = ((), (), s32[]{:S(2)}) async-start(), calls=%async_computation | async-start | bytes 20971520 | tf_op jit(solution)/shard_map/psum | solution.py:9
  36.1 642.9 %all-reduce.7.cloned.1.call-start = ((), (), s32[]{:S(2)}) async-start(), calls=%async_computation.2 | async-start | bytes 18874368 | tf_op jit(solution)/shard_map/psum | solution.py:9
  473.2 6.1 copy-start
Sparse Core Ops, SparseCore 0:
  24.9 122.7 all-gather.1
  510.6 168.3 all-reduce.6
Sparse Core Ops, SparseCore 1:
  36.2 330.4 all-reduce.4
